TPU v7x, 1024 devices: a whole 4x4x32 slice. The times are simulated.
1024 devices in a mesh: gx: 16 (over y_lo, x, core), gz: 64 (over z, y_hi).
Axes of the slice: x: 4, y: 4 (y_hi: 2, y_lo: 2; y = y_hi * 2 + y_lo), z: 32, core: 2. Of those that a mesh axis runs over, the one named last changes fastest.
Arguments:
- conserved: float32 [5, 64, 256, 128], P(None, 'gx', 'gz'), may hold values from -1.1 to 5.5, as said below
- jacobian: float32 [64, 256, 128], P('gx', 'gz'), may hold values from 0.5 to 2
- metric: float32 [3, 3, 64, 256, 128], P(None, None, 'gx', 'gz'), may hold values from -0.45 to 2.01, as said below
- x_master: int32 [32, 64, 32], P('gx', 'gz'), may hold values from 0 to 1, as said below
- x_flip: int32 [32, 64, 32], P('gx', 'gz'), may hold values from 0 to 7, as said below
- z_master: int32 [16, 128, 32], P('gx', 'gz'), may hold values from 0 to 1, as said below
- z_flip: int32 [16, 128, 32], P('gx', 'gz'), may hold values from 0 to 7, as said below
Outputs:
- rhs: float32 [5, 64, 256, 128], P(None, 'gx', 'gz')
Inputs may be any that keep to these rules, and one draw needn't show every extreme that they name: conserved[0] is at least 0.6, and the pressure 0.4 (conserved[4] - 0.5 |conserved[1:4]|^2 / conserved[0]) is at least 0.6. metric[g, g] lies between 0.49 and 2.01; every other entry has magnitude at most 0.45. `x_master`: rows 2 t and 2 t + 1 hold the faces on the lower and upper streamwise boundary of tile t; 1 marks that tile t holds the master side. Row 2 t + 1 equals 1 minus row 2 t + 2 (rows taken cyclically), so each face has exactly one master. `x_flip`: rows as in x_master; row 2 t + 1 equals row 2 t + 2 (rows taken cyclically). `z_master`: columns 2 t and 2 t + 1 hold the faces on the lower and upper spanwise boundary of tile t; 1 marks that tile t holds the master side. Column 2 t + 1 equals 1 minus column 2 t + 2 (taken cyclically). `z_flip`: columns as in z_master; column 2 t + 1 equals column 2 t + 2 (taken cyclically).
All inputs are finite; a program needn't handle non-finite values.
Results may differ from a plain program's by a relative error of at most 0.0003.
Values sent between devices are 32-bit elements; how exact they have to be, the bound alone decides.
A program may use at most 64 MiB of HBM per device.

v0:
```python
import functools
import math

import jax
import jax.numpy as jnp
import numpy as np
from jax import lax
from jax.experimental import pallas as pl
from jax.experimental.pallas import tpu as pltpu
from jax.sharding import PartitionSpec as P

MESH = pl.DeviceIdType.MESH
gamma_gas = 1.4
visc_coef = 0.1
prandtl = 0.72
heat_ratio = gamma_gas / ((gamma_gas - 1.0) * prandtl)


def node_table():
    points = np.array([-1.0, -math.sqrt(0.2), math.sqrt(0.2), 1.0])
    scales = np.array(
        [np.prod([points[r] - points[s] for s in range(4) if s != r]) for r in range(4)]
    )
    table = np.zeros((4, 4))
    for r in range(4):
        for c in range(4):
            if r != c:
                table[r, c] = scales[r] / (scales[c] * (points[r] - points[c]))
        table[r, r] = -np.sum(table[r])
    return table


weak = node_table()
weak[0, 0] += 6.0
weak[3, 3] -= 6.0


def pick(index, values):
    result = jnp.full(index.shape, float(values[3]), jnp.float32)
    for at in range(3):
        result = jnp.where(index == at, float(values[at]), result)
    return result


def along(values, index, axis):
    shape = values.shape
    flat = values.reshape((-1, 8, 128))
    parts = [
        jnp.take_along_axis(flat[n], index, axis=axis, mode="promise_in_bounds")
        for n in range(flat.shape[0])
    ]
    return jnp.stack(parts).reshape(shape)


def primitives(state):
    inverse = 1.0 / state[0]
    velocity = [state[1 + j] * inverse for j in range(3)]
    kinetic = state[1] * velocity[0] + state[2] * velocity[1] + state[3] * velocity[2]
    pressure = (gamma_gas - 1.0) * (state[4] - 0.5 * kinetic)
    return velocity, pressure, pressure * inverse


def dot3(left, right):
    return left[0] * right[0] + left[1] * right[1] + left[2] * right[2]


def fluxes(state, velocity, pressure, slopes):
    third = (2.0 / 3.0) * (slopes[0][0] + slopes[1][1] + slopes[2][2])
    stress = [[None] * 3 for _ in range(3)]
    moment = [[None] * 3 for _ in range(3)]
    for j in range(3):
        for d in range(j, 3):
            tau = slopes[j][d] + slopes[d][j]
            flow = state[1 + j] * velocity[d]
            if j == d:
                tau = tau - third
                flow = flow + pressure
            stress[j][d] = stress[d][j] = tau
            moment[j][d] = moment[d][j] = flow - tau
    total = state[4] + pressure
    energy = [
        total * velocity[d] - dot3(velocity, stress[d]) - heat_ratio * slopes[3][d]
        for d in range(3)
    ]
    return moment, energy


def wave(velocity, sound, normal, size):
    return jnp.abs(dot3(velocity, normal)) + sound * size


def kernel(
    nx, nz, cons_n, met_n, jac_n, cons_f, met_f, xm, xf, zm, zf, out,
    nodes, metv, jacv, face, recv1, send2, recv2, codes, lsem, csem, s1, r1, s2, r2,
):
    gx, gz = lax.axis_index("gx"), lax.axis_index("gz")
    x_up, x_low = lax.rem(gx + 1, nx), lax.rem(gx + nx - 1, nx)
    z_up, z_low = lax.rem(gz + 1, nz), lax.rem(gz + nz - 1, nz)
    targets = [(x_up, gz), (x_low, gz), (gx, z_up), (gx, z_low)]

    barrier = pltpu.get_barrier_semaphore()
    for target in targets:
        pl.semaphore_signal(barrier, inc=1, device_id=target, device_id_type=MESH)

    low, up = pl.ds(0, 4), pl.ds(4, 4)
    five, three = pl.ds(0, 5), pl.ds(5, 3)
    packs = [
        (cons_f.at[:, 0], face.at[0, five, low]),
        (cons_f.at[:, 3], face.at[0, five, up]),
        (met_f.at[0, :, 0], face.at[0, three, low]),
        (met_f.at[0, :, 3], face.at[0, three, up]),
        (cons_f.at[:, :, 0, :], face.at[1, five, low]),
        (cons_f.at[:, :, 3, :], face.at[1, five, up]),
        (met_f.at[1, :, :, 0, :], face.at[1, three, low]),
        (met_f.at[1, :, :, 3, :], face.at[1, three, up]),
    ]
    packs = [pltpu.make_async_copy(a, b, lsem.at[n]) for n, (a, b) in enumerate(packs)]
    loads = [(cons_n, nodes), (met_n, metv), (jac_n, jacv)]
    loads += [(ref, codes.at[n]) for n, ref in enumerate((xm, xf, zm, zf))]
    loads = [pltpu.make_async_copy(a, b, csem.at[n]) for n, (a, b) in enumerate(loads)]
    for copy in packs + loads:
        copy.start()

    sub = lax.broadcasted_iota(jnp.int32, (8, 128), 0)
    lane = lax.broadcasted_iota(jnp.int32, (8, 128), 1)
    row, col = sub & 3, lane & 3
    lower = sub < 4
    half = sub >> 2
    side = jnp.where(lower, -1.0, 1.0)
    x_node = [jnp.where(lower, 1.0, 0.0), jnp.where(lower, 0.0, 1.0)]
    z_edge = jnp.where((row == 0) | (row == 3), 1.0, 0.0)
    cross_index = half * 3 + jnp.where(row == 3, 4, 0)
    z_index = half + jnp.where(row == 3, 4, 0)
    z_from = ((sub & 1) << 2) + half * 3
    z_first = row < 2
    cz = [pick(row, [weak[a, a ^ s] for a in range(4)]) for s in range(4)]
    cy = [pick(col, [weak[a, a ^ s] for a in range(4)]) for s in range(4)]
    cx = [
        [
            [
                jnp.where(lower, float(weak[2 * v, 2 * w + s]), float(weak[2 * v + 1, 2 * w + 1 - s]))
                for s in range(2)
            ]
            for w in range(2)
        ]
        for v in range(2)
    ]
    wall = (lane == 0) | (lane == 127)
    wall_sign = jnp.where(wall, -1.0, 1.0)
    y_other = jnp.where(
        wall, lane, jnp.where(col == 0, lane - 1, jnp.where(col == 3, lane + 1, lane))
    )
    y_lead = jnp.where((col == 0) & (lane > 0), lane - 1, lane)
    y_side = jnp.where(col == 0, -3.0, jnp.where(col == 3, 3.0, 0.0))
    y_jump = jnp.abs(y_side)

    def d_x(v):
        r = jnp.stack([pltpu.roll(v[n], 4, 1) for n in range(v.shape[0])])
        parts = [
            cx[n][0][0] * v[:, 0] + cx[n][0][1] * r[:, 0] + cx[n][1][0] * v[:, 1] + cx[n][1][1] * r[:, 1]
            for n in range(2)
        ]
        return jnp.stack(parts, 1)

    def d_z(v):
        result = cz[0] * v
        for s in range(1, 4):
            result = result + cz[s] * along(v, sub ^ s, 0)
        return result

    def d_y(v):
        result = cy[0] * v
        for s in range(1, 4):
            result = result + cy[s] * along(v, lane ^ s, 1)
        return result

    def to_faces(v):
        ends = along(v, z_from, 0)
        return jnp.stack([jnp.where(lower, v[0], v[1]), jnp.where(z_first, ends[0], ends[1])])

    def to_nodes(f):
        z0 = along(f[1], z_index, 0)
        z1 = along(f[1], z_index + 2, 0)
        return jnp.stack([f[0] * x_node[0] + z0 * z_edge, f[0] * x_node[1] + z1 * z_edge])

    for copy in packs:
        copy.wait()
    pl.semaphore_wait(barrier, 4)
    sends1 = []
    for n, target in enumerate(targets):
        axis, from_up = n // 2, n % 2 == 0
        sends1.append(
            pltpu.make_async_remote_copy(
                src_ref=face.at[axis, :, up if from_up else low],
                dst_ref=recv1.at[axis, :, low if from_up else up],
                send_sem=s1.at[n],
                recv_sem=r1.at[n],
                device_id=target,
                device_id_type=MESH,
            )
        )
    for copy in sends1:
        copy.start()

    for copy in loads:
        copy.wait()
    lead, lane_one, row_two, lane_three = [], [], [], []
    for axis in range(2):
        word = codes[2 * axis + 1] + 8 * codes[2 * axis]
        word = jnp.where(
            lax.broadcasted_iota(jnp.int32, (8, 32), 0) < 4,
            jnp.broadcast_to(word[0:1], (8, 32)),
            jnp.broadcast_to(word[1:2], (8, 32)),
        )
        word = along(jnp.concatenate([word] * 4, 1), lane >> 2, 1)
        first, second = (word & 1) * 3, ((word >> 1) & 1) * 3
        swap = (word & 4) != 0
        lead.append((word & 8) != 0)
        lane_one.append(lane ^ jnp.where(swap, row ^ first ^ second, second))
        row_two.append(
            sub ^ jnp.where(swap, col ^ jnp.where(lower, first, second), first)
        )
        lane_three.append(lane ^ jnp.where(swap, row, 0))

    def orient(axis, layer):
        layer = along(layer, lane_one[axis], 1)
        layer = along(layer, row_two[axis], 0)
        return along(layer, lane_three[axis], 1)

    state = [nodes[k] for k in range(5)]
    metric = [[metv[g, d] for d in range(3)] for g in range(3)]
    velocity, pressure, warm = primitives(state)
    lifted = jnp.stack(velocity + [warm])
    inverse_j = 1.0 / jacv[...]

    def products(g):
        return (lifted[:, None] * jnp.stack(metric[g])[None]).reshape(12, 2, 8, 128)

    partial = d_x(products(0)) + d_z(products(1)) + d_y(products(2))
    y_normal = [along(metric[2][d], y_lead, 1) for d in range(3)]
    y_sums = [
        y_side * (lifted[k] + (wall_sign if k < 3 else 1.0) * along(lifted[k], y_other, 1))
        for k in range(4)
    ]
    partial = [
        [partial[3 * k + d] + y_sums[k] * y_normal[d] for d in range(3)] for k in range(4)
    ]
    scaled = visc_coef * inverse_j
    face_partial = [[to_faces(partial[k][d]) for d in range(3)] for k in range(4)]
    face_scaled = to_faces(scaled)
    own = [face[:, k] for k in range(8)]
    own_velocity, own_pressure, own_warm = primitives(own)
    own_lifted = own_velocity + [own_warm]

    for copy in sends1:
        copy.wait_recv()
    other = [
        jnp.stack([orient(axis, recv1[axis, k]) for axis in range(2)]) for k in range(8)
    ]
    leads = jnp.stack(lead)
    normal = [jnp.where(leads, own[5 + d], other[5 + d]) for d in range(3)]
    other_velocity, other_pressure, other_warm = primitives(other)
    other_lifted = other_velocity + [other_warm]
    sums = [(3.0 * side) * (own_lifted[k] + other_lifted[k]) for k in range(4)]

    def crossed(f):
        return jnp.stack([along(f[1], cross_index, 0), along(f[0], cross_index, 0)])

    cross_sums = [z_edge * crossed(sums[k]) for k in range(4)]
    cross_normal = [crossed(normal[d]) for d in range(3)]
    face_slopes = [
        [
            face_scaled
            * (face_partial[k][d] + sums[k] * normal[d] + cross_sums[k] * cross_normal[d])
            for d in range(3)
        ]
        for k in range(4)
    ]
    moment, energy = fluxes(own, own_velocity, own_pressure, face_slopes)
    own_half = [dot3(moment[j], normal) for j in range(3)] + [dot3(energy, normal)]
    for k in range(4):
        send2[:, k] = own_half[k]

    sends2 = []
    for n, target in enumerate(targets):
        axis, from_up = n // 2, n % 2 == 0
        sends2.append(
            pltpu.make_async_remote_copy(
                src_ref=send2.at[axis, :, up if from_up else low],
                dst_ref=recv2.at[axis, :, low if from_up else up],
                send_sem=s2.at[n],
                recv_sem=r2.at[n],
                device_id=target,
                device_id_type=MESH,
            )
        )
    for copy in sends2:
        copy.start()

    z_sums = [jnp.stack([along(sums[k][1], z_index, 0), along(sums[k][1], z_index + 2, 0)]) * z_edge for k in range(4)]
    z_normal = [jnp.stack([along(normal[d][1], z_index, 0), along(normal[d][1], z_index + 2, 0)]) for d in range(3)]
    x_mask = jnp.stack(x_node)
    slopes = [
        [
            scaled
            * (
                partial[k][d]
                + x_mask * (sums[k][0] * normal[d][0])
                + z_sums[k] * z_normal[d]
            )
            for d in range(3)
        ]
        for k in range(4)
    ]
    moment, energy = fluxes(state, velocity, pressure, slopes)

    def through(rows):
        parts = [dot3(state[1:4], rows)]
        parts += [dot3(moment[j], rows) for j in range(3)]
        return parts + [dot3(energy, rows)]

    total = d_x(jnp.stack(through(metric[0])))
    total = total + d_z(jnp.stack(through(metric[1])))
    total = total + d_y(jnp.stack(through(metric[2])))

    half_y = through(y_normal)
    heat_y = (-2.0 * heat_ratio) * dot3(slopes[3], y_normal)
    size_y = jnp.sqrt(dot3(y_normal, y_normal))
    speed = wave(velocity, jnp.sqrt(gamma_gas * warm), y_normal, size_y)
    speed = y_jump * jnp.maximum(speed, along(speed, y_other, 1))
    y_terms = []
    for k in range(5):
        sign = wall_sign if 1 <= k <= 3 else 1.0
        jump = sign * along(state[k], y_other, 1) - state[k]
        sign = wall_sign if k == 0 else 1.0
        both = half_y[k] + sign * along(half_y[k], y_other, 1)
        if k == 4:
            both = jnp.where(wall, heat_y, both)
        y_terms.append(y_side * both - speed * jump)

    size = jnp.sqrt(dot3(normal, normal))
    speed = jnp.maximum(
        wave(own_velocity, jnp.sqrt(gamma_gas * own_warm), normal, size),
        wave(other_velocity, jnp.sqrt(gamma_gas * other_warm), normal, size),
    )
    known = [dot3([own[1 + d] + other[1 + d] for d in range(3)], normal)] + own_half
    known = [
        (3.0 * side) * known[k] - (3.0 * speed) * (other[k] - own[k]) for k in range(5)
    ]
    out[0] = -inverse_j * (total[0] + y_terms[0] + to_nodes(known[0]))
    rest = [total[k] + y_terms[k] + to_nodes(known[k]) for k in range(1, 5)]

    for copy in sends2:
        copy.wait_recv()
    for k in range(4):
        arrived = jnp.stack([orient(axis, recv2[axis, k]) for axis in range(2)])
        out[1 + k] = -inverse_j * (rest[k] + to_nodes((3.0 * side) * arrived))
    for copy in sends1 + sends2:
        copy.wait_send()


def local(nx, nz, conserved, jacobian, metric, x_master, x_flip, z_master, z_flip):
    anywhere = pl.BlockSpec(memory_space=pl.ANY)
    words = [v.reshape(2, 32) for v in (x_master, x_flip, z_master, z_flip)]
    result = pl.pallas_call(
        functools.partial(kernel, nx, nz),
        out_shape=jax.ShapeDtypeStruct((5, 2, 8, 128), jnp.float32),
        in_specs=[anywhere] * 9,
        out_specs=pl.BlockSpec(memory_space=pltpu.VMEM),
        scratch_shapes=[
            pltpu.VMEM((5, 2, 8, 128), jnp.float32),
            pltpu.VMEM((3, 3, 2, 8, 128), jnp.float32),
            pltpu.VMEM((2, 8, 128), jnp.float32),
            pltpu.VMEM((2, 8, 8, 128), jnp.float32),
            pltpu.VMEM((2, 8, 8, 128), jnp.float32),
            pltpu.VMEM((2, 4, 8, 128), jnp.float32),
            pltpu.VMEM((2, 4, 8, 128), jnp.float32),
            pltpu.VMEM((4, 2, 32), jnp.int32),
            pltpu.SemaphoreType.DMA((8,)),
            pltpu.SemaphoreType.DMA((7,)),
            pltpu.SemaphoreType.DMA((4,)),
            pltpu.SemaphoreType.DMA((4,)),
            pltpu.SemaphoreType.DMA((4,)),
            pltpu.SemaphoreType.DMA((4,)),
        ],
        compiler_params=pltpu.CompilerParams(collective_id=0, has_side_effects=True),
    )(
        conserved.reshape(5, 2, 8, 128),
        metric.reshape(3, 3, 2, 8, 128),
        jacobian.reshape(2, 8, 128),
        conserved,
        metric,
        *words,
    )
    return result.reshape(5, 4, 4, 128)


def solution(mesh):
    flags = P("gx", "gz", None)
    in_specs = (P(None, "gx", "gz", None), flags, P(None, None, "gx", "gz", None)) + (flags,) * 4
    return jax.shard_map(
        functools.partial(local, mesh.shape["gx"], mesh.shape["gz"]),
        mesh=mesh,
        in_specs=in_specs,
        out_specs=P(None, "gx", "gz", None),
        check_vma=False,
    )
```

profile of v0, /device:TPU:6, one launch (start us, length us, event | category | flops | bytes accessed | tf_op | source)
XLA Modules:
  0.0 31.9 jit_solution(8364694266554655963)
XLA Ops:
  0.0 30.4 %shard_map.73 = f32[5,2,8,128]{3,2,1,0:T(8,128)} custom-call(f32[5,2,8,128]{3,2,1,0:T(8,128)} %bitcast.9, f32[3,3,2,8,128]{4,3,2,1,0:T(8,128)} %bitcast.8, f32[2,8,128]{2,1,0:T(8,128)} %bitcast.11, f32[5,4,4,128]{3,2,1,0:T(4,128)} %cons_f.1, f32[3,3,4,4,128]{4,3,2,1,0:T(4,128)} %met_f.1, s32[2,32]{1,0:T(2,128)} %bitcast.12, s32[2,32]{1,0:T(2,128)} %bitcast.13, ...), custom_call_target="tpu_custom_call" | custom-call | tf_op jit(solution)/shard_map/pallas_call | solution.py:365
  30.5 1.4 %copy.9 = f32[5,4,4,128]{3,2,1,0:T(4,128)} copy(f32[5,4,4,128]{3,2,1,0:T(4,128)} %bitcast.10) | data formatting | bytes 81920
where the time goes:
time: 32.1 us; the launch traced here: 31.9 us
  Pallas kernels  30.4 us (95%)
  local copies, waits for them, and re-layouts  1.4 us (4%)
    pallas_call x1, Pallas kernels, local(): pl.pallas_call(functools.partial(kernel, nx, nz), out_shape=jax.ShapeDtyp...  30.4 us
    unnamed x1, local copies, waits for them, and re-layouts  1.4 us

commit v1 on v0

--- a/solution.py
+++ b/solution.py
@@ -364,7 +364,7 @@
     words = [v.reshape(2, 32) for v in (x_master, x_flip, z_master, z_flip)]
     result = pl.pallas_call(
         functools.partial(kernel, nx, nz),
-        out_shape=jax.ShapeDtypeStruct((5, 2, 8, 128), jnp.float32),
+        out_shape=pltpu.VMEM((5, 2, 8, 128), jnp.float32),
         in_specs=[anywhere] * 9,
         out_specs=pl.BlockSpec(memory_space=pltpu.VMEM),
         scratch_shapes=[

time: 32.1 us -> 30.6 us (0.953)
  local copies, waits for them, and re-layouts: 1.4 us -> 0.62 us
  Pallas kernels: 30.4 us -> 29.8 us
    unnamed x1, local copies, waits for them, and re-layouts: 1.4 us -> 0.62 us
    pallas_call x1, Pallas kernels: 30.4 us -> 29.8 us  [local(): pl.pallas_call(functools.partial(kernel, nx, nz), out_shape=pltpu.VMEM((5...]
where the time goes in v1:
time: 30.6 us; the launch traced here: 30.5 us
  Pallas kernels  29.8 us (97%)
  local copies, waits for them, and re-layouts  0.62 us (2%)
    pallas_call x1, Pallas kernels, local(): pl.pallas_call(functools.partial(kernel, nx, nz), out_shape=pltpu.VMEM((5...  29.8 us
    unnamed x1, local copies, waits for them, and re-layouts  0.62 us

profile of v1, /device:TPU:6, one launch (start us, length us, event | category | flops | bytes accessed | tf_op | source)
XLA Modules:
  0.0 30.5 jit_solution(13604301431339156867)
XLA Ops:
  0.0 29.8 %shard_map.73 = f32[5,2,8,128]{3,2,1,0:T(8,128)S(1)} custom-call(f32[5,2,8,128]{3,2,1,0:T(8,128)} %bitcast.10, f32[3,3,2,8,128]{4,3,2,1,0:T(8,128)} %bitcast.9, f32[2,8,128]{2,1,0:T(8,128)} %bitcast.11, f32[5,4,4,128]{3,2,1,0:T(4,128)} %cons_f.1, f32[3,3,4,4,128]{4,3,2,1,0:T(4,128)} %met_f.1, s32[2,32]{1,0:T(2,128)} %bitcast.12, s32[2,32]{1,0:T(2,128)} %bitcast.13, ...), custom_call_target="tpu_custom_call" | custom-call | tf_op jit(solution)/shard_map/pallas_call | solution.py:365
  29.8 0.6 %copy.9 = f32[5,4,4,128]{3,2,1,0:T(4,128)} copy(f32[5,4,4,128]{3,2,1,0:T(4,128)S(1)} %bitcast.8) | data formatting | bytes 81920

commit v2 on v1

--- a/solution.py
+++ b/solution.py
@@ -91,19 +91,25 @@
 
 def kernel(
     nx, nz, cons_n, met_n, jac_n, cons_f, met_f, xm, xf, zm, zf, out,
-    nodes, metv, jacv, face, recv1, send2, recv2, codes, lsem, csem, s1, r1, s2, r2,
+    nodes, metv, jacv, face, recv, edge, corner, codes, lsem, csem, ssem, rsem,
 ):
     gx, gz = lax.axis_index("gx"), lax.axis_index("gz")
-    x_up, x_low = lax.rem(gx + 1, nx), lax.rem(gx + nx - 1, nx)
-    z_up, z_low = lax.rem(gz + 1, nz), lax.rem(gz + nz - 1, nz)
-    targets = [(x_up, gz), (x_low, gz), (gx, z_up), (gx, z_low)]
-
+    x_to = [lax.rem(gx + nx - 1, nx), gx, lax.rem(gx + 1, nx)]
+    z_to = [lax.rem(gz + nz - 1, nz), gz, lax.rem(gz + 1, nz)]
+    sides = [(1, 0), (-1, 0), (0, 1), (0, -1)]
+    diagonals = [(1, 1), (1, -1), (-1, 1), (-1, -1)]
+    target = lambda way: (x_to[way[0] + 1], z_to[way[1] + 1])
+
+    corner[...] = jnp.zeros_like(corner)
     barrier = pltpu.get_barrier_semaphore()
-    for target in targets:
-        pl.semaphore_signal(barrier, inc=1, device_id=target, device_id_type=MESH)
+    for way in sides + diagonals:
+        pl.semaphore_signal(barrier, inc=1, device_id=target(way), device_id_type=MESH)
 
     low, up = pl.ds(0, 4), pl.ds(4, 4)
     five, three = pl.ds(0, 5), pl.ds(5, 3)
+    loads = [(cons_n, nodes), (met_n, metv), (jac_n, jacv)]
+    loads += [(ref, codes.at[n]) for n, ref in enumerate((xm, xf, zm, zf))]
+    loads = [pltpu.make_async_copy(a, b, csem.at[n]) for n, (a, b) in enumerate(loads)]
     packs = [
         (cons_f.at[:, 0], face.at[0, five, low]),
         (cons_f.at[:, 3], face.at[0, five, up]),
@@ -115,10 +121,7 @@
         (met_f.at[1, :, :, 3, :], face.at[1, three, up]),
     ]
     packs = [pltpu.make_async_copy(a, b, lsem.at[n]) for n, (a, b) in enumerate(packs)]
-    loads = [(cons_n, nodes), (met_n, metv), (jac_n, jacv)]
-    loads += [(ref, codes.at[n]) for n, ref in enumerate((xm, xf, zm, zf))]
-    loads = [pltpu.make_async_copy(a, b, csem.at[n]) for n, (a, b) in enumerate(loads)]
-    for copy in packs + loads:
+    for copy in loads + packs:
         copy.start()
 
     sub = lax.broadcasted_iota(jnp.int32, (8, 128), 0)
@@ -153,6 +156,7 @@
     y_lead = jnp.where((col == 0) & (lane > 0), lane - 1, lane)
     y_side = jnp.where(col == 0, -3.0, jnp.where(col == 3, 3.0, 0.0))
     y_jump = jnp.abs(y_side)
+    edge_side = jnp.where(row == 0, -3.0, jnp.where(row == 3, 3.0, 0.0))
 
     def d_x(v):
         r = jnp.stack([pltpu.roll(v[n], 4, 1) for n in range(v.shape[0])])
@@ -183,49 +187,40 @@
         z1 = along(f[1], z_index + 2, 0)
         return jnp.stack([f[0] * x_node[0] + z0 * z_edge, f[0] * x_node[1] + z1 * z_edge])
 
-    for copy in packs:
-        copy.wait()
-    pl.semaphore_wait(barrier, 4)
-    sends1 = []
-    for n, target in enumerate(targets):
-        axis, from_up = n // 2, n % 2 == 0
-        sends1.append(
-            pltpu.make_async_remote_copy(
-                src_ref=face.at[axis, :, up if from_up else low],
-                dst_ref=recv1.at[axis, :, low if from_up else up],
-                send_sem=s1.at[n],
-                recv_sem=r1.at[n],
-                device_id=target,
-                device_id_type=MESH,
-            )
-        )
-    for copy in sends1:
-        copy.start()
+    def crossed(f):
+        return along(f, cross_index, 0)
 
     for copy in loads:
         copy.wait()
-    lead, lane_one, row_two, lane_three = [], [], [], []
+    lead, lead_edge, lane_one, row_in, row_out, lane_three = [], [], [], [], [], []
+    rows_at = lax.broadcasted_iota(jnp.int32, (8, 32), 0)
     for axis in range(2):
         word = codes[2 * axis + 1] + 8 * codes[2 * axis]
-        word = jnp.where(
-            lax.broadcasted_iota(jnp.int32, (8, 32), 0) < 4,
-            jnp.broadcast_to(word[0:1], (8, 32)),
-            jnp.broadcast_to(word[1:2], (8, 32)),
-        )
+        first = jnp.broadcast_to(word[0:1], (8, 32))
+        second = jnp.broadcast_to(word[1:2], (8, 32))
+        cross = jnp.where((rows_at & 3) < 2, first, second)
+        word = jnp.where(rows_at < 4, first, second)
+        cross = along(jnp.concatenate([cross] * 4, 1), lane >> 2, 1)
         word = along(jnp.concatenate([word] * 4, 1), lane >> 2, 1)
         first, second = (word & 1) * 3, ((word >> 1) & 1) * 3
         swap = (word & 4) != 0
-        lead.append((word & 8) != 0)
+        lead.append(word >> 3)
+        lead_edge.append(cross >> 3)
         lane_one.append(lane ^ jnp.where(swap, row ^ first ^ second, second))
-        row_two.append(
-            sub ^ jnp.where(swap, col ^ jnp.where(lower, first, second), first)
-        )
+        row_in.append(sub ^ jnp.where(swap, col ^ jnp.where(lower, first, second), first))
+        row_out.append(sub ^ jnp.where(swap, col ^ jnp.where(lower, second, first), first))
         lane_three.append(lane ^ jnp.where(swap, row, 0))
-
-    def orient(axis, layer):
-        layer = along(layer, lane_one[axis], 1)
-        layer = along(layer, row_two[axis], 0)
-        return along(layer, lane_three[axis], 1)
+    lead = jnp.stack(lead).astype(jnp.float32)
+    leads = lead > 0.5
+    lead_edge = jnp.stack(lead_edge[::-1]).astype(jnp.float32)
+
+    def orient(layers, row_two):
+        parts = []
+        for axis in range(2):
+            layer = along(layers[axis], lane_one[axis], 1)
+            layer = along(layer, row_two[axis], 0)
+            parts.append(along(layer, lane_three[axis], 1))
+        return jnp.stack(parts)
 
     state = [nodes[k] for k in range(5)]
     metric = [[metv[g, d] for d in range(3)] for g in range(3)]
@@ -242,72 +237,124 @@
         y_side * (lifted[k] + (wall_sign if k < 3 else 1.0) * along(lifted[k], y_other, 1))
         for k in range(4)
     ]
+    scaled = visc_coef * inverse_j
     partial = [
-        [partial[3 * k + d] + y_sums[k] * y_normal[d] for d in range(3)] for k in range(4)
-    ]
-    scaled = visc_coef * inverse_j
+        [scaled * (partial[3 * k + d] + y_sums[k] * y_normal[d]) for d in range(3)]
+        for k in range(4)
+    ]
     face_partial = [[to_faces(partial[k][d]) for d in range(3)] for k in range(4)]
     face_scaled = to_faces(scaled)
+    for k in range(4):
+        for d in range(3):
+            face[:, 8 + 3 * k + d] = face_partial[k][d]
+    face[:, 20] = face_scaled
+    for d in range(3):
+        across = to_faces(metric[1][d])[0], to_faces(metric[0][d])[1]
+        face[:, 21 + d] = lead_edge * jnp.stack(across)
+
+    for copy in packs:
+        copy.wait()
     own = [face[:, k] for k in range(8)]
     own_velocity, own_pressure, own_warm = primitives(own)
     own_lifted = own_velocity + [own_warm]
-
-    for copy in sends1:
+    seen = [orient(v, row_out) for v in own_lifted + [lead * own[5 + d] for d in range(3)]]
+    for k in range(7):
+        edge[0, k] = crossed(seen[k][0])
+        edge[1, k] = seen[k][1]
+
+    pl.semaphore_wait(barrier, 8)
+    sends = []
+    for n, way in enumerate(sides):
+        axis, from_up = n // 2, n % 2 == 0
+        sends.append(
+            pltpu.make_async_remote_copy(
+                src_ref=face.at[axis, :, up if from_up else low],
+                dst_ref=recv.at[axis, :, low if from_up else up],
+                send_sem=ssem.at[n],
+                recv_sem=rsem.at[n],
+                device_id=target(way),
+                device_id_type=MESH,
+            )
+        )
+    for n, way in enumerate(diagonals):
+        at = (3 if way[0] > 0 else 0) + (4 if way[1] > 0 else 0)
+        sends.append(
+            pltpu.make_async_remote_copy(
+                src_ref=edge.at[:, :, pl.ds(at, 1)],
+                dst_ref=corner.at[:, :, pl.ds(7 - at, 1)],
+                send_sem=ssem.at[4 + n],
+                recv_sem=rsem.at[4 + n],
+                device_id=target(way),
+                device_id_type=MESH,
+            )
+        )
+    for copy in sends[4:] + sends[:4]:
+        copy.start()
+    for copy in sends:
         copy.wait_recv()
-    other = [
-        jnp.stack([orient(axis, recv1[axis, k]) for axis in range(2)]) for k in range(8)
-    ]
-    leads = jnp.stack(lead)
-    normal = [jnp.where(leads, own[5 + d], other[5 + d]) for d in range(3)]
-    other_velocity, other_pressure, other_warm = primitives(other)
-    other_lifted = other_velocity + [other_warm]
-    sums = [(3.0 * side) * (own_lifted[k] + other_lifted[k]) for k in range(4)]
-
-    def crossed(f):
-        return jnp.stack([along(f[1], cross_index, 0), along(f[0], cross_index, 0)])
-
-    cross_sums = [z_edge * crossed(sums[k]) for k in range(4)]
-    cross_normal = [crossed(normal[d]) for d in range(3)]
-    face_slopes = [
+
+    they = [recv[:, k] for k in range(8)]
+    they_scaled = recv[:, 20]
+    they_velocity, they_pressure, they_warm = primitives(they)
+    they_lifted = they_velocity + [they_warm]
+    they_normal = [jnp.where(leads, seen[4 + d], they[5 + d]) for d in range(3)]
+    they_sums = [(-3.0 * side) * (they_lifted[k] + seen[k]) for k in range(4)]
+    line = [jnp.stack([crossed(corner[1, k]), corner[0, k]]) for k in range(7)]
+    line_sums = [edge_side * (they_lifted[k] + line[k]) for k in range(4)]
+    line_normal = [recv[:, 21 + d] + line[4 + d] for d in range(3)]
+    they_slopes = [
         [
-            face_scaled
-            * (face_partial[k][d] + sums[k] * normal[d] + cross_sums[k] * cross_normal[d])
+            recv[:, 8 + 3 * k + d]
+            + they_scaled * (they_sums[k] * they_normal[d] + line_sums[k] * line_normal[d])
             for d in range(3)
         ]
         for k in range(4)
     ]
+    moment, energy = fluxes(they, they_velocity, they_pressure, they_slopes)
+    they_half = [dot3(they[1:4], they_normal)]
+    they_half += [dot3(moment[j], they_normal) for j in range(3)]
+    they_half += [dot3(energy, they_normal)]
+    they_size = jnp.sqrt(dot3(they_normal, they_normal))
+    they_speed = wave(they_velocity, jnp.sqrt(gamma_gas * they_warm), they_normal, they_size)
+
+    other = [orient(they[k], row_in) for k in range(5)]
+    other_half = [orient(they_half[k], row_in) for k in range(5)]
+    other_speed = orient(they_speed, row_in)
+    sums = [-orient(they_sums[k], row_in) for k in range(4)]
+    normal = [jnp.where(leads, own[5 + d], orient(they[5 + d], row_in)) for d in range(3)]
+
+    def both_crossed(f):
+        return jnp.stack([crossed(f[1]), crossed(f[0])])
+
+    cross_sums = [z_edge * both_crossed(sums[k]) for k in range(4)]
+    cross_normal = [both_crossed(normal[d]) for d in range(3)]
+    face_slopes = [
+        [
+            face_partial[k][d]
+            + face_scaled * (sums[k] * normal[d] + cross_sums[k] * cross_normal[d])
+            for d in range(3)
+        ]
+        for k in range(4)
+    ]
     moment, energy = fluxes(own, own_velocity, own_pressure, face_slopes)
-    own_half = [dot3(moment[j], normal) for j in range(3)] + [dot3(energy, normal)]
-    for k in range(4):
-        send2[:, k] = own_half[k]
-
-    sends2 = []
-    for n, target in enumerate(targets):
-        axis, from_up = n // 2, n % 2 == 0
-        sends2.append(
-            pltpu.make_async_remote_copy(
-                src_ref=send2.at[axis, :, up if from_up else low],
-                dst_ref=recv2.at[axis, :, low if from_up else up],
-                send_sem=s2.at[n],
-                recv_sem=r2.at[n],
-                device_id=target,
-                device_id_type=MESH,
-            )
-        )
-    for copy in sends2:
-        copy.start()
+    own_half = [dot3(own[1:4], normal)]
+    own_half += [dot3(moment[j], normal) for j in range(3)] + [dot3(energy, normal)]
+    own_speed = wave(
+        own_velocity, jnp.sqrt(gamma_gas * own_warm), normal, jnp.sqrt(dot3(normal, normal))
+    )
+    speed = 3.0 * jnp.maximum(own_speed, other_speed)
+    tile_terms = [
+        (3.0 * side) * (own_half[k] + other_half[k]) - speed * (other[k] - own[k])
+        for k in range(5)
+    ]
 
     z_sums = [jnp.stack([along(sums[k][1], z_index, 0), along(sums[k][1], z_index + 2, 0)]) * z_edge for k in range(4)]
     z_normal = [jnp.stack([along(normal[d][1], z_index, 0), along(normal[d][1], z_index + 2, 0)]) for d in range(3)]
     x_mask = jnp.stack(x_node)
     slopes = [
         [
-            scaled
-            * (
-                partial[k][d]
-                + x_mask * (sums[k][0] * normal[d][0])
-                + z_sums[k] * z_normal[d]
-            )
+            partial[k][d]
+            + scaled * (x_mask * (sums[k][0] * normal[d][0]) + z_sums[k] * z_normal[d])
             for d in range(3)
         ]
         for k in range(4)
@@ -338,24 +385,9 @@
             both = jnp.where(wall, heat_y, both)
         y_terms.append(y_side * both - speed * jump)
 
-    size = jnp.sqrt(dot3(normal, normal))
-    speed = jnp.maximum(
-        wave(own_velocity, jnp.sqrt(gamma_gas * own_warm), normal, size),
-        wave(other_velocity, jnp.sqrt(gamma_gas * other_warm), normal, size),
-    )
-    known = [dot3([own[1 + d] + other[1 + d] for d in range(3)], normal)] + own_half
-    known = [
-        (3.0 * side) * known[k] - (3.0 * speed) * (other[k] - own[k]) for k in range(5)
-    ]
-    out[0] = -inverse_j * (total[0] + y_terms[0] + to_nodes(known[0]))
-    rest = [total[k] + y_terms[k] + to_nodes(known[k]) for k in range(1, 5)]
-
-    for copy in sends2:
-        copy.wait_recv()
-    for k in range(4):
-        arrived = jnp.stack([orient(axis, recv2[axis, k]) for axis in range(2)])
-        out[1 + k] = -inverse_j * (rest[k] + to_nodes((3.0 * side) * arrived))
-    for copy in sends1 + sends2:
+    for k in range(5):
+        out[k] = -inverse_j * (total[k] + y_terms[k] + to_nodes(tile_terms[k]))
+    for copy in sends:
         copy.wait_send()
 
 
@@ -371,17 +403,15 @@
             pltpu.VMEM((5, 2, 8, 128), jnp.float32),
             pltpu.VMEM((3, 3, 2, 8, 128), jnp.float32),
             pltpu.VMEM((2, 8, 128), jnp.float32),
-            pltpu.VMEM((2, 8, 8, 128), jnp.float32),
-            pltpu.VMEM((2, 8, 8, 128), jnp.float32),
-            pltpu.VMEM((2, 4, 8, 128), jnp.float32),
-            pltpu.VMEM((2, 4, 8, 128), jnp.float32),
+            pltpu.VMEM((2, 24, 8, 128), jnp.float32),
+            pltpu.VMEM((2, 24, 8, 128), jnp.float32),
+            pltpu.VMEM((2, 7, 8, 128), jnp.float32),
+            pltpu.VMEM((2, 7, 8, 128), jnp.float32),
             pltpu.VMEM((4, 2, 32), jnp.int32),
             pltpu.SemaphoreType.DMA((8,)),
             pltpu.SemaphoreType.DMA((7,)),
-            pltpu.SemaphoreType.DMA((4,)),
-            pltpu.SemaphoreType.DMA((4,)),
-            pltpu.SemaphoreType.DMA((4,)),
-            pltpu.SemaphoreType.DMA((4,)),
+            pltpu.SemaphoreType.DMA((8,)),
+            pltpu.SemaphoreType.DMA((8,)),
         ],
         compiler_params=pltpu.CompilerParams(collective_id=0, has_side_effects=True),
     )(

time: 30.6 us -> 27.1 us (0.89)
  the two profiles are of different devices: /device:TPU:6 before, /device:TPU:1 now
where the time goes in v2:
time: 27.1 us; the launch traced here: 27 us
  Pallas kernels  26.3 us (97%)
  local copies, waits for them, and re-layouts  0.62 us (2%)
    pallas_call x1, Pallas kernels, local(): pl.pallas_call(functools.partial(kernel, nx, nz), out_shape=pltpu.VMEM((5...  26.3 us
    unnamed x1, local copies, waits for them, and re-layouts  0.62 us

profile of v2, /device:TPU:1, one launch (start us, length us, event | category | flops | bytes accessed | tf_op | source)
XLA Modules:
  0.0 27.0 jit_solution(7296119890291738658)
XLA Ops:
  0.0 26.3 %shard_map.73 = f32[5,2,8,128]{3,2,1,0:T(8,128)S(1)} custom-call(f32[5,2,8,128]{3,2,1,0:T(8,128)} %bitcast.10, f32[3,3,2,8,128]{4,3,2,1,0:T(8,128)} %bitcast.9, f32[2,8,128]{2,1,0:T(8,128)} %bitcast.11, f32[5,4,4,128]{3,2,1,0:T(4,128)} %cons_f.1, f32[3,3,4,4,128]{4,3,2,1,0:T(4,128)} %met_f.1, s32[2,32]{1,0:T(2,128)} %bitcast.12, s32[2,32]{1,0:T(2,128)} %bitcast.13, ...), custom_call_target="tpu_custom_call" | custom-call | tf_op jit(solution)/shard_map/pallas_call | solution.py:397
  26.3 0.6 %copy.9 = f32[5,4,4,128]{3,2,1,0:T(4,128)} copy(f32[5,4,4,128]{3,2,1,0:T(4,128)S(1)} %bitcast.8) | data formatting | bytes 81920

commit v3 on v2

--- a/solution.py
+++ b/solution.py
@@ -64,22 +64,29 @@
     return left[0] * right[0] + left[1] * right[1] + left[2] * right[2]
 
 
-def fluxes(state, velocity, pressure, slopes):
+def flows(state, velocity, pressure):
+    moment = [[None] * 3 for _ in range(3)]
+    for j in range(3):
+        for d in range(j, 3):
+            flow = state[1 + j] * velocity[d]
+            moment[j][d] = moment[d][j] = flow + pressure if j == d else flow
+    total = state[4] + pressure
+    return moment, [total * velocity[d] for d in range(3)]
+
+
+def fluxes(inviscid, velocity, slopes):
     third = (2.0 / 3.0) * (slopes[0][0] + slopes[1][1] + slopes[2][2])
     stress = [[None] * 3 for _ in range(3)]
     moment = [[None] * 3 for _ in range(3)]
     for j in range(3):
         for d in range(j, 3):
             tau = slopes[j][d] + slopes[d][j]
-            flow = state[1 + j] * velocity[d]
             if j == d:
                 tau = tau - third
-                flow = flow + pressure
             stress[j][d] = stress[d][j] = tau
-            moment[j][d] = moment[d][j] = flow - tau
-    total = state[4] + pressure
+            moment[j][d] = moment[d][j] = inviscid[0][j][d] - tau
     energy = [
-        total * velocity[d] - dot3(velocity, stress[d]) - heat_ratio * slopes[3][d]
+        inviscid[1][d] - dot3(velocity, stress[d]) - heat_ratio * slopes[3][d]
         for d in range(3)
     ]
     return moment, energy
@@ -90,8 +97,8 @@
 
 
 def kernel(
-    nx, nz, cons_n, met_n, jac_n, cons_f, met_f, xm, xf, zm, zf, out,
-    nodes, metv, jacv, face, recv, edge, corner, codes, lsem, csem, ssem, rsem,
+    nx, nz, cons_n, met_n, jac_n, xm, xf, zm, zf, out,
+    nodes, metv, jacv, face, recv, edge, corner, codes, csem, ssem, rsem,
 ):
     gx, gz = lax.axis_index("gx"), lax.axis_index("gz")
     x_to = [lax.rem(gx + nx - 1, nx), gx, lax.rem(gx + 1, nx)]
@@ -102,26 +109,14 @@
 
     corner[...] = jnp.zeros_like(corner)
     barrier = pltpu.get_barrier_semaphore()
-    for way in sides + diagonals:
+    for way in diagonals + sides[::-1]:
         pl.semaphore_signal(barrier, inc=1, device_id=target(way), device_id_type=MESH)
 
     low, up = pl.ds(0, 4), pl.ds(4, 4)
-    five, three = pl.ds(0, 5), pl.ds(5, 3)
-    loads = [(cons_n, nodes), (met_n, metv), (jac_n, jacv)]
-    loads += [(ref, codes.at[n]) for n, ref in enumerate((xm, xf, zm, zf))]
+    loads = [(ref, codes.at[n]) for n, ref in enumerate((xm, xf, zm, zf))]
+    loads += [(cons_n, nodes), (met_n, metv), (jac_n, jacv)]
     loads = [pltpu.make_async_copy(a, b, csem.at[n]) for n, (a, b) in enumerate(loads)]
-    packs = [
-        (cons_f.at[:, 0], face.at[0, five, low]),
-        (cons_f.at[:, 3], face.at[0, five, up]),
-        (met_f.at[0, :, 0], face.at[0, three, low]),
-        (met_f.at[0, :, 3], face.at[0, three, up]),
-        (cons_f.at[:, :, 0, :], face.at[1, five, low]),
-        (cons_f.at[:, :, 3, :], face.at[1, five, up]),
-        (met_f.at[1, :, :, 0, :], face.at[1, three, low]),
-        (met_f.at[1, :, :, 3, :], face.at[1, three, up]),
-    ]
-    packs = [pltpu.make_async_copy(a, b, lsem.at[n]) for n, (a, b) in enumerate(packs)]
-    for copy in loads + packs:
+    for copy in loads:
         copy.start()
 
     sub = lax.broadcasted_iota(jnp.int32, (8, 128), 0)
@@ -190,7 +185,7 @@
     def crossed(f):
         return along(f, cross_index, 0)
 
-    for copy in loads:
+    for copy in loads[:4]:
         copy.wait()
     lead, lead_edge, lane_one, row_in, row_out, lane_three = [], [], [], [], [], []
     rows_at = lax.broadcasted_iota(jnp.int32, (8, 32), 0)
@@ -222,11 +217,39 @@
             parts.append(along(layer, lane_three[axis], 1))
         return jnp.stack(parts)
 
+    loads[4].wait()
     state = [nodes[k] for k in range(5)]
-    metric = [[metv[g, d] for d in range(3)] for g in range(3)]
     velocity, pressure, warm = primitives(state)
     lifted = jnp.stack(velocity + [warm])
-    inverse_j = 1.0 / jacv[...]
+    own_velocity = [to_faces(v) for v in velocity]
+    own_warm = to_faces(warm)
+    own_lifted = own_velocity + [own_warm]
+    loads[5].wait()
+    metric = [[metv[g, d] for d in range(3)] for g in range(3)]
+    own_row = [
+        jnp.stack([to_faces(metric[0][d])[0], to_faces(metric[1][d])[1]]) for d in range(3)
+    ]
+    seen = [orient(v, row_out) for v in own_lifted + [lead * own_row[d] for d in range(3)]]
+    for k in range(7):
+        edge[0, k] = crossed(seen[k][0])
+        edge[1, k] = seen[k][1]
+
+    pl.semaphore_wait(barrier, 8)
+    corner_sends = []
+    for n, way in enumerate(diagonals):
+        at = (3 if way[0] > 0 else 0) + (4 if way[1] > 0 else 0)
+        corner_sends.append(
+            pltpu.make_async_remote_copy(
+                src_ref=edge.at[:, :, pl.ds(at, 1)],
+                dst_ref=corner.at[:, :, pl.ds(7 - at, 1)],
+                send_sem=ssem.at[4 + n],
+                recv_sem=rsem.at[4 + n],
+                device_id=target(way),
+                device_id_type=MESH,
+            )
+        )
+    for copy in corner_sends:
+        copy.start()
 
     def products(g):
         return (lifted[:, None] * jnp.stack(metric[g])[None]).reshape(12, 2, 8, 128)
@@ -237,6 +260,8 @@
         y_side * (lifted[k] + (wall_sign if k < 3 else 1.0) * along(lifted[k], y_other, 1))
         for k in range(4)
     ]
+    loads[6].wait()
+    inverse_j = 1.0 / jacv[...]
     scaled = visc_coef * inverse_j
     partial = [
         [scaled * (partial[3 * k + d] + y_sums[k] * y_normal[d]) for d in range(3)]
@@ -244,6 +269,11 @@
     ]
     face_partial = [[to_faces(partial[k][d]) for d in range(3)] for k in range(4)]
     face_scaled = to_faces(scaled)
+    own = [to_faces(state[k]) for k in range(5)]
+    for k in range(5):
+        face[:, k] = own[k]
+    for d in range(3):
+        face[:, 5 + d] = own_row[d]
     for k in range(4):
         for d in range(3):
             face[:, 8 + 3 * k + d] = face_partial[k][d]
@@ -252,17 +282,6 @@
         across = to_faces(metric[1][d])[0], to_faces(metric[0][d])[1]
         face[:, 21 + d] = lead_edge * jnp.stack(across)
 
-    for copy in packs:
-        copy.wait()
-    own = [face[:, k] for k in range(8)]
-    own_velocity, own_pressure, own_warm = primitives(own)
-    own_lifted = own_velocity + [own_warm]
-    seen = [orient(v, row_out) for v in own_lifted + [lead * own[5 + d] for d in range(3)]]
-    for k in range(7):
-        edge[0, k] = crossed(seen[k][0])
-        edge[1, k] = seen[k][1]
-
-    pl.semaphore_wait(barrier, 8)
     sends = []
     for n, way in enumerate(sides):
         axis, from_up = n // 2, n % 2 == 0
@@ -276,20 +295,25 @@
                 device_id_type=MESH,
             )
         )
-    for n, way in enumerate(diagonals):
-        at = (3 if way[0] > 0 else 0) + (4 if way[1] > 0 else 0)
-        sends.append(
-            pltpu.make_async_remote_copy(
-                src_ref=edge.at[:, :, pl.ds(at, 1)],
-                dst_ref=corner.at[:, :, pl.ds(7 - at, 1)],
-                send_sem=ssem.at[4 + n],
-                recv_sem=rsem.at[4 + n],
-                device_id=target(way),
-                device_id_type=MESH,
-            )
-        )
-    for copy in sends[4:] + sends[:4]:
+    for copy in sends[::-1]:
         copy.start()
+
+    inviscid = flows(state, velocity, pressure)
+    own_inviscid = flows(own, own_velocity, to_faces(pressure))
+    own_sound = jnp.sqrt(gamma_gas * own_warm)
+    size_y = jnp.sqrt(dot3(y_normal, y_normal))
+    speed = wave(velocity, jnp.sqrt(gamma_gas * warm), y_normal, size_y)
+    speed = y_jump * jnp.maximum(speed, along(speed, y_other, 1))
+    y_terms = []
+    for k in range(5):
+        sign = wall_sign if 1 <= k <= 3 else 1.0
+        y_terms.append(speed * (state[k] - sign * along(state[k], y_other, 1)))
+    mass_y = dot3(state[1:4], y_normal)
+    mass_terms = y_terms[0] + y_side * (mass_y + wall_sign * along(mass_y, y_other, 1))
+    mass_flux = [dot3(state[1:4], metric[g])[None] for g in range(3)]
+    mass_terms = mass_terms + (d_x(mass_flux[0]) + d_z(mass_flux[1]) + d_y(mass_flux[2]))[0]
+    mass_terms = -inverse_j * mass_terms
+
     for copy in sends:
         copy.wait_recv()
 
@@ -299,18 +323,16 @@
     they_lifted = they_velocity + [they_warm]
     they_normal = [jnp.where(leads, seen[4 + d], they[5 + d]) for d in range(3)]
     they_sums = [(-3.0 * side) * (they_lifted[k] + seen[k]) for k in range(4)]
-    line = [jnp.stack([crossed(corner[1, k]), corner[0, k]]) for k in range(7)]
-    line_sums = [edge_side * (they_lifted[k] + line[k]) for k in range(4)]
-    line_normal = [recv[:, 21 + d] + line[4 + d] for d in range(3)]
     they_slopes = [
         [
             recv[:, 8 + 3 * k + d]
-            + they_scaled * (they_sums[k] * they_normal[d] + line_sums[k] * line_normal[d])
+            + (they_scaled * they_sums[k]) * they_normal[d]
             for d in range(3)
         ]
         for k in range(4)
     ]
-    moment, energy = fluxes(they, they_velocity, they_pressure, they_slopes)
+    they_inviscid = flows(they, they_velocity, they_pressure)
+    moment, energy = fluxes(they_inviscid, they_velocity, they_slopes)
     they_half = [dot3(they[1:4], they_normal)]
     they_half += [dot3(moment[j], they_normal) for j in range(3)]
     they_half += [dot3(energy, they_normal)]
@@ -321,7 +343,7 @@
     other_half = [orient(they_half[k], row_in) for k in range(5)]
     other_speed = orient(they_speed, row_in)
     sums = [-orient(they_sums[k], row_in) for k in range(4)]
-    normal = [jnp.where(leads, own[5 + d], orient(they[5 + d], row_in)) for d in range(3)]
+    normal = [jnp.where(leads, own_row[d], orient(they[5 + d], row_in)) for d in range(3)]
 
     def both_crossed(f):
         return jnp.stack([crossed(f[1]), crossed(f[0])])
@@ -336,12 +358,10 @@
         ]
         for k in range(4)
     ]
-    moment, energy = fluxes(own, own_velocity, own_pressure, face_slopes)
+    moment, energy = fluxes(own_inviscid, own_velocity, face_slopes)
     own_half = [dot3(own[1:4], normal)]
     own_half += [dot3(moment[j], normal) for j in range(3)] + [dot3(energy, normal)]
-    own_speed = wave(
-        own_velocity, jnp.sqrt(gamma_gas * own_warm), normal, jnp.sqrt(dot3(normal, normal))
-    )
+    own_speed = wave(own_velocity, own_sound, normal, jnp.sqrt(dot3(normal, normal)))
     speed = 3.0 * jnp.maximum(own_speed, other_speed)
     tile_terms = [
         (3.0 * side) * (own_half[k] + other_half[k]) - speed * (other[k] - own[k])
@@ -359,12 +379,10 @@
         ]
         for k in range(4)
     ]
-    moment, energy = fluxes(state, velocity, pressure, slopes)
+    moment, energy = fluxes(inviscid, velocity, slopes)
 
     def through(rows):
-        parts = [dot3(state[1:4], rows)]
-        parts += [dot3(moment[j], rows) for j in range(3)]
-        return parts + [dot3(energy, rows)]
+        return [dot3(moment[j], rows) for j in range(3)] + [dot3(energy, rows)]
 
     total = d_x(jnp.stack(through(metric[0])))
     total = total + d_z(jnp.stack(through(metric[1])))
@@ -372,22 +390,35 @@
 
     half_y = through(y_normal)
     heat_y = (-2.0 * heat_ratio) * dot3(slopes[3], y_normal)
-    size_y = jnp.sqrt(dot3(y_normal, y_normal))
-    speed = wave(velocity, jnp.sqrt(gamma_gas * warm), y_normal, size_y)
-    speed = y_jump * jnp.maximum(speed, along(speed, y_other, 1))
-    y_terms = []
-    for k in range(5):
-        sign = wall_sign if 1 <= k <= 3 else 1.0
-        jump = sign * along(state[k], y_other, 1) - state[k]
-        sign = wall_sign if k == 0 else 1.0
-        both = half_y[k] + sign * along(half_y[k], y_other, 1)
-        if k == 4:
+    for k in range(4):
+        both = half_y[k] + along(half_y[k], y_other, 1)
+        if k == 3:
             both = jnp.where(wall, heat_y, both)
-        y_terms.append(y_side * both - speed * jump)
-
-    for k in range(5):
-        out[k] = -inverse_j * (total[k] + y_terms[k] + to_nodes(tile_terms[k]))
-    for copy in sends:
+        y_terms[1 + k] = y_terms[1 + k] + y_side * both
+    out[0] = mass_terms - inverse_j * to_nodes(tile_terms[0])
+    ready = [
+        -inverse_j * (total[k] + y_terms[1 + k] + to_nodes(tile_terms[1 + k])) for k in range(4)
+    ]
+
+    for copy in corner_sends:
+        copy.wait_recv()
+    line = [jnp.stack([crossed(corner[1, k]), corner[0, k]]) for k in range(7)]
+    line_sums = [
+        (edge_side * they_scaled) * (they_lifted[k] + line[k]) for k in range(4)
+    ]
+    line_normal = [recv[:, 21 + d] + line[4 + d] for d in range(3)]
+    onto = dot3(line_normal, they_normal)
+    carried = dot3(line_sums, they_normal)
+    spread = (2.0 / 3.0) * dot3(line_sums, line_normal)
+    drag = [
+        spread * they_normal[j] - line_sums[j] * onto - line_normal[j] * carried
+        for j in range(3)
+    ]
+    drag.append(dot3(they_velocity, drag) - heat_ratio * (line_sums[3] * onto))
+    for k in range(4):
+        late = (3.0 * side) * orient(drag[k], row_in)
+        out[1 + k] = ready[k] - inverse_j * to_nodes(late)
+    for copy in sends + corner_sends:
         copy.wait_send()
 
 
@@ -397,7 +428,7 @@
     result = pl.pallas_call(
         functools.partial(kernel, nx, nz),
         out_shape=pltpu.VMEM((5, 2, 8, 128), jnp.float32),
-        in_specs=[anywhere] * 9,
+        in_specs=[anywhere] * 7,
         out_specs=pl.BlockSpec(memory_space=pltpu.VMEM),
         scratch_shapes=[
             pltpu.VMEM((5, 2, 8, 128), jnp.float32),
@@ -408,7 +439,6 @@
             pltpu.VMEM((2, 7, 8, 128), jnp.float32),
             pltpu.VMEM((2, 7, 8, 128), jnp.float32),
             pltpu.VMEM((4, 2, 32), jnp.int32),
-            pltpu.SemaphoreType.DMA((8,)),
             pltpu.SemaphoreType.DMA((7,)),
             pltpu.SemaphoreType.DMA((8,)),
             pltpu.SemaphoreType.DMA((8,)),
@@ -418,8 +448,6 @@
         conserved.reshape(5, 2, 8, 128),
         metric.reshape(3, 3, 2, 8, 128),
         jacobian.reshape(2, 8, 128),
-        conserved,
-        metric,
         *words,
     )
     return result.reshape(5, 4, 4, 128)

time: 27.1 us -> 26.8 us (0.989)
  Pallas kernels: 26.3 us -> 26 us
    pallas_call x1, Pallas kernels: 26.3 us -> 26 us  [local(): pl.pallas_call(functools.partial(kernel, nx, nz), out_shape=pltpu.VMEM((5...]
where the time goes in v3:
time: 26.8 us; the launch traced here: 26.6 us
  Pallas kernels  26 us (97%)
  local copies, waits for them, and re-layouts  0.62 us (2%)
    pallas_call x1, Pallas kernels, local(): pl.pallas_call(functools.partial(kernel, nx, nz), out_shape=pltpu.VMEM((5...  26 us
    unnamed x1, local copies, waits for them, and re-layouts  0.62 us

profile of v3, /device:TPU:1, one launch (start us, length us, event | category | flops | bytes accessed | tf_op | source)
XLA Modules:
  0.0 26.6 jit_solution(316984443585659905)
XLA Ops:
  0.0 26.0 %shard_map.73 = f32[5,2,8,128]{3,2,1,0:T(8,128)S(1)} custom-call(f32[5,2,8,128]{3,2,1,0:T(8,128)} %bitcast.10, f32[3,3,2,8,128]{4,3,2,1,0:T(8,128)} %bitcast.9, f32[2,8,128]{2,1,0:T(8,128)} %bitcast.11, s32[2,32]{1,0:T(2,128)} %bitcast.12, s32[2,32]{1,0:T(2,128)} %bitcast.13, s32[2,32]{1,0:T(2,128)} %bitcast.14, s32[2,32]{1,0:T(2,128)} %bitcast.15), custom_call_target="tpu_custom_call" | custom-call | tf_op jit(solution)/shard_map/pallas_call | solution.py:428
  26.0 0.6 %copy.9 = f32[5,4,4,128]{3,2,1,0:T(4,128)} copy(f32[5,4,4,128]{3,2,1,0:T(4,128)S(1)} %bitcast.8) | data formatting | bytes 81920

commit v4 on v3

--- a/solution.py
+++ b/solution.py
@@ -98,7 +98,7 @@
 
 def kernel(
     nx, nz, cons_n, met_n, jac_n, xm, xf, zm, zf, out,
-    nodes, metv, jacv, face, recv, edge, corner, codes, csem, ssem, rsem,
+    nodes, metv, jacv, face, recv, edge, corner, codes, csem, ssem, rsem, ready,
 ):
     gx, gz = lax.axis_index("gx"), lax.axis_index("gz")
     x_to = [lax.rem(gx + nx - 1, nx), gx, lax.rem(gx + 1, nx)]
@@ -107,18 +107,28 @@
     diagonals = [(1, 1), (1, -1), (-1, 1), (-1, -1)]
     target = lambda way: (x_to[way[0] + 1], z_to[way[1] + 1])
 
-    corner[...] = jnp.zeros_like(corner)
-    barrier = pltpu.get_barrier_semaphore()
-    for way in diagonals + sides[::-1]:
-        pl.semaphore_signal(barrier, inc=1, device_id=target(way), device_id_type=MESH)
-
-    low, up = pl.ds(0, 4), pl.ds(4, 4)
     loads = [(ref, codes.at[n]) for n, ref in enumerate((xm, xf, zm, zf))]
     loads += [(cons_n, nodes), (met_n, metv), (jac_n, jacv)]
     loads = [pltpu.make_async_copy(a, b, csem.at[n]) for n, (a, b) in enumerate(loads)]
     for copy in loads:
         copy.start()
 
+    corner[...] = jnp.zeros_like(corner)
+    even = lax.rem(gz, 2) == 0
+    barrier = pltpu.get_barrier_semaphore()
+    for way in ((1, -1), (-1, -1), (0, -1)):
+        pl.semaphore_signal(barrier, inc=1, device_id=target(way), device_id_type=MESH)
+
+    @pl.when(even)
+    def _():
+        for way in ((1, 0), (-1, 0)):
+            pl.semaphore_signal(barrier, inc=1, device_id=target(way), device_id_type=MESH)
+
+    pl.semaphore_wait(barrier, 5 - 2 * lax.rem(gz, 2))
+    for way in ((1, 1), (-1, 1), (0, 1)):
+        pl.semaphore_signal(ready, inc=1, device_id=target(way), device_id_type=MESH)
+
+    low, up = pl.ds(0, 4), pl.ds(4, 4)
     sub = lax.broadcasted_iota(jnp.int32, (8, 128), 0)
     lane = lax.broadcasted_iota(jnp.int32, (8, 128), 1)
     row, col = sub & 3, lane & 3
@@ -234,7 +244,6 @@
         edge[0, k] = crossed(seen[k][0])
         edge[1, k] = seen[k][1]
 
-    pl.semaphore_wait(barrier, 8)
     corner_sends = []
     for n, way in enumerate(diagonals):
         at = (3 if way[0] > 0 else 0) + (4 if way[1] > 0 else 0)
@@ -248,8 +257,8 @@
                 device_id_type=MESH,
             )
         )
-    for copy in corner_sends:
-        copy.start()
+    corner_sends[0].start()
+    corner_sends[2].start()
 
     def products(g):
         return (lifted[:, None] * jnp.stack(metric[g])[None]).reshape(12, 2, 8, 128)
@@ -295,8 +304,22 @@
                 device_id_type=MESH,
             )
         )
-    for copy in sends[::-1]:
-        copy.start()
+    sends[2].start()
+
+    @pl.when(even)
+    def _():
+        sends[0].start()
+        sends[1].start()
+
+    pl.semaphore_wait(ready, 3)
+    corner_sends[1].start()
+    corner_sends[3].start()
+    sends[3].start()
+
+    @pl.when(jnp.logical_not(even))
+    def _():
+        sends[0].start()
+        sends[1].start()
 
     inviscid = flows(state, velocity, pressure)
     own_inviscid = flows(own, own_velocity, to_faces(pressure))
@@ -442,6 +465,7 @@
             pltpu.SemaphoreType.DMA((7,)),
             pltpu.SemaphoreType.DMA((8,)),
             pltpu.SemaphoreType.DMA((8,)),
+            pltpu.SemaphoreType.REGULAR,
         ],
         compiler_params=pltpu.CompilerParams(collective_id=0, has_side_effects=True),
     )(

time: 26.8 us -> 26.2 us (0.978)
  Pallas kernels: 26 us -> 25.4 us
    pallas_call x1, Pallas kernels: 26 us -> 25.4 us  [local(): pl.pallas_call(functools.partial(kernel, nx, nz), out_shape=pltpu.VMEM((5...]
where the time goes in v4:
time: 26.2 us; the launch traced here: 26 us
  Pallas kernels  25.4 us (97%)
  local copies, waits for them, and re-layouts  0.62 us (2%)
    pallas_call x1, Pallas kernels, local(): pl.pallas_call(functools.partial(kernel, nx, nz), out_shape=pltpu.VMEM((5...  25.4 us
    unnamed x1, local copies, waits for them, and re-layouts  0.62 us

profile of v4, /device:TPU:1, one launch (start us, length us, event | category | flops | bytes accessed | tf_op | source)
XLA Modules:
  0.0 26.0 jit_solution(15909733363970200141)
XLA Ops:
  0.0 25.4 %shard_map.73 = f32[5,2,8,128]{3,2,1,0:T(8,128)S(1)} custom-call(f32[5,2,8,128]{3,2,1,0:T(8,128)} %bitcast.10, f32[3,3,2,8,128]{4,3,2,1,0:T(8,128)} %bitcast.9, f32[2,8,128]{2,1,0:T(8,128)} %bitcast.11, s32[2,32]{1,0:T(2,128)} %bitcast.12, s32[2,32]{1,0:T(2,128)} %bitcast.13, s32[2,32]{1,0:T(2,128)} %bitcast.14, s32[2,32]{1,0:T(2,128)} %bitcast.15), custom_call_target="tpu_custom_call" | custom-call | tf_op jit(solution)/shard_map/pallas_call | solution.py:451
  25.4 0.6 %copy.9 = f32[5,4,4,128]{3,2,1,0:T(4,128)} copy(f32[5,4,4,128]{3,2,1,0:T(4,128)S(1)} %bitcast.8) | data formatting | bytes 81920

commit v5 on v3

--- a/solution.py
+++ b/solution.py
@@ -97,8 +97,8 @@
 
 
 def kernel(
-    nx, nz, cons_n, met_n, jac_n, xm, xf, zm, zf, out,
-    nodes, metv, jacv, face, recv, edge, corner, codes, csem, ssem, rsem,
+    nx, nz, cons_n, met_n, jac_n, cons_f, met_f, xm, xf, zm, zf, out,
+    nodes, metv, jacv, face, recv, corner, words, theirs, codes, csem, ssem, rsem, ready,
 ):
     gx, gz = lax.axis_index("gx"), lax.axis_index("gz")
     x_to = [lax.rem(gx + nx - 1, nx), gx, lax.rem(gx + 1, nx)]
@@ -107,12 +107,49 @@
     diagonals = [(1, 1), (1, -1), (-1, 1), (-1, -1)]
     target = lambda way: (x_to[way[0] + 1], z_to[way[1] + 1])
 
-    corner[...] = jnp.zeros_like(corner)
+    even = lax.rem(gz, 2) == 0
     barrier = pltpu.get_barrier_semaphore()
-    for way in diagonals + sides[::-1]:
+    for way in ((1, -1), (-1, -1), (0, -1)):
         pl.semaphore_signal(barrier, inc=1, device_id=target(way), device_id_type=MESH)
 
+    @pl.when(even)
+    def _():
+        for way in ((1, 0), (-1, 0)):
+            pl.semaphore_signal(barrier, inc=1, device_id=target(way), device_id_type=MESH)
+
+    pl.semaphore_wait(barrier, 5 - 2 * lax.rem(gz, 2))
+    for way in ((1, 1), (-1, 1), (0, 1)):
+        pl.semaphore_signal(ready, inc=1, device_id=target(way), device_id_type=MESH)
+
     low, up = pl.ds(0, 4), pl.ds(4, 4)
+    five, three = pl.ds(0, 5), pl.ds(5, 3)
+    corner_sends = []
+    for n, way in enumerate(diagonals):
+        x_at, z_at = (3 if way[0] > 0 else 0), (3 if way[1] > 0 else 0)
+        x_from, z_from_ = (0 if way[0] > 0 else 1), (0 if way[1] > 0 else 1)
+        x_rows, z_rows = (low, up)[x_from], (low, up)[z_from_]
+        pairs = [
+            (cons_f.at[:, :, z_at, :], corner.at[0, x_from, five, z_rows]),
+            (met_f.at[1, :, :, z_at, :], corner.at[0, x_from, three, z_rows]),
+            (cons_f.at[:, x_at], corner.at[1, z_from_, five, x_rows]),
+            (met_f.at[0, :, x_at], corner.at[1, z_from_, three, x_rows]),
+        ]
+        for m, (source, place) in enumerate(pairs):
+            corner_sends.append(
+                pltpu.make_async_remote_copy(
+                    src_ref=source,
+                    dst_ref=place,
+                    send_sem=ssem.at[8 + 4 * n + m],
+                    recv_sem=rsem.at[8 + 4 * n + m],
+                    device_id=target(way),
+                    device_id_type=MESH,
+                )
+            )
+    corner_next = corner_sends[0:4] + corner_sends[8:12]
+    corner_previous = corner_sends[4:8] + corner_sends[12:16]
+    for copy in corner_next:
+        copy.start()
+
     loads = [(ref, codes.at[n]) for n, ref in enumerate((xm, xf, zm, zf))]
     loads += [(cons_n, nodes), (met_n, metv), (jac_n, jacv)]
     loads = [pltpu.make_async_copy(a, b, csem.at[n]) for n, (a, b) in enumerate(loads)]
@@ -199,6 +236,7 @@
         word = along(jnp.concatenate([word] * 4, 1), lane >> 2, 1)
         first, second = (word & 1) * 3, ((word >> 1) & 1) * 3
         swap = (word & 4) != 0
+        words[axis] = word
         lead.append(word >> 3)
         lead_edge.append(cross >> 3)
         lane_one.append(lane ^ jnp.where(swap, row ^ first ^ second, second))
@@ -230,27 +268,6 @@
         jnp.stack([to_faces(metric[0][d])[0], to_faces(metric[1][d])[1]]) for d in range(3)
     ]
     seen = [orient(v, row_out) for v in own_lifted + [lead * own_row[d] for d in range(3)]]
-    for k in range(7):
-        edge[0, k] = crossed(seen[k][0])
-        edge[1, k] = seen[k][1]
-
-    pl.semaphore_wait(barrier, 8)
-    corner_sends = []
-    for n, way in enumerate(diagonals):
-        at = (3 if way[0] > 0 else 0) + (4 if way[1] > 0 else 0)
-        corner_sends.append(
-            pltpu.make_async_remote_copy(
-                src_ref=edge.at[:, :, pl.ds(at, 1)],
-                dst_ref=corner.at[:, :, pl.ds(7 - at, 1)],
-                send_sem=ssem.at[4 + n],
-                recv_sem=rsem.at[4 + n],
-                device_id=target(way),
-                device_id_type=MESH,
-            )
-        )
-    for copy in corner_sends:
-        copy.start()
-
     def products(g):
         return (lifted[:, None] * jnp.stack(metric[g])[None]).reshape(12, 2, 8, 128)
 
@@ -295,8 +312,32 @@
                 device_id_type=MESH,
             )
         )
-    for copy in sends[::-1]:
+        sends.append(
+            pltpu.make_async_remote_copy(
+                src_ref=words.at[1 - axis],
+                dst_ref=theirs.at[axis, 0 if from_up else 1],
+                send_sem=ssem.at[4 + n],
+                recv_sem=rsem.at[4 + n],
+                device_id=target(way),
+                device_id_type=MESH,
+            )
+        )
+    for copy in sends[4:6]:
         copy.start()
+
+    @pl.when(even)
+    def _():
+        for copy in sends[0:4]:
+            copy.start()
+
+    pl.semaphore_wait(ready, 3)
+    for copy in corner_previous + sends[6:8]:
+        copy.start()
+
+    @pl.when(jnp.logical_not(even))
+    def _():
+        for copy in sends[0:4]:
+            copy.start()
 
     inviscid = flows(state, velocity, pressure)
     own_inviscid = flows(own, own_velocity, to_faces(pressure))
@@ -400,9 +441,40 @@
         -inverse_j * (total[k] + y_terms[1 + k] + to_nodes(tile_terms[1 + k])) for k in range(4)
     ]
 
+    wanted = jnp.where(lower, jnp.where(row == 3, 7, 3), jnp.where(row == 3, 4, 0))
+    turn_one, turn_row, turn_three, turn_mask = [], [], [], []
+    for axis in range(2):
+        ones, rows, swaps, masks = [], [], [], []
+        for h in range(2):
+            word = theirs[axis, h]
+            first, second = (word & 1) * 3, ((word >> 1) & 1) * 3
+            ones.append(lane ^ jnp.where((word & 4) != 0, row ^ first ^ second, second))
+            word = along(word, wanted, 0)
+            first, second = (word & 1) * 3, ((word >> 1) & 1) * 3
+            swap = (word & 4) != 0
+            turned = col ^ jnp.where(wanted < 4, first, second)
+            rows.append(wanted ^ jnp.where(swap, turned, first))
+            swaps.append(jnp.where(swap, wanted & 3, 0))
+            masks.append(1 - (word >> 3))
+        turn_one.append(ones)
+        turn_row.append(rows)
+        turn_three.append(lane ^ jnp.where(lower, swaps[0], swaps[1]))
+        turn_mask.append(jnp.where(lower, masks[0], masks[1]).astype(jnp.float32))
+    turn_mask = jnp.stack(turn_mask)
+
     for copy in corner_sends:
         copy.wait_recv()
-    line = [jnp.stack([crossed(corner[1, k]), corner[0, k]]) for k in range(7)]
+    met = [[] for _ in range(8)]
+    for axis in range(2):
+        for k in range(8):
+            parts = [
+                along(along(corner[axis, h, k], turn_one[axis][h], 1), turn_row[axis][h], 0)
+                for h in range(2)
+            ]
+            met[k].append(along(jnp.where(lower, parts[0], parts[1]), turn_three[axis], 1))
+    met = [jnp.stack(v) for v in met]
+    met_velocity, _, met_warm = primitives(met)
+    line = met_velocity + [met_warm] + [turn_mask * met[5 + d] for d in range(3)]
     line_sums = [
         (edge_side * they_scaled) * (they_lifted[k] + line[k]) for k in range(4)
     ]
@@ -428,7 +500,7 @@
     result = pl.pallas_call(
         functools.partial(kernel, nx, nz),
         out_shape=pltpu.VMEM((5, 2, 8, 128), jnp.float32),
-        in_specs=[anywhere] * 7,
+        in_specs=[anywhere] * 9,
         out_specs=pl.BlockSpec(memory_space=pltpu.VMEM),
         scratch_shapes=[
             pltpu.VMEM((5, 2, 8, 128), jnp.float32),
@@ -436,18 +508,22 @@
             pltpu.VMEM((2, 8, 128), jnp.float32),
             pltpu.VMEM((2, 24, 8, 128), jnp.float32),
             pltpu.VMEM((2, 24, 8, 128), jnp.float32),
-            pltpu.VMEM((2, 7, 8, 128), jnp.float32),
-            pltpu.VMEM((2, 7, 8, 128), jnp.float32),
+            pltpu.VMEM((2, 2, 8, 8, 128), jnp.float32),
+            pltpu.VMEM((2, 8, 128), jnp.int32),
+            pltpu.VMEM((2, 2, 8, 128), jnp.int32),
             pltpu.VMEM((4, 2, 32), jnp.int32),
             pltpu.SemaphoreType.DMA((7,)),
-            pltpu.SemaphoreType.DMA((8,)),
-            pltpu.SemaphoreType.DMA((8,)),
+            pltpu.SemaphoreType.DMA((24,)),
+            pltpu.SemaphoreType.DMA((24,)),
+            pltpu.SemaphoreType.REGULAR,
         ],
         compiler_params=pltpu.CompilerParams(collective_id=0, has_side_effects=True),
     )(
         conserved.reshape(5, 2, 8, 128),
         metric.reshape(3, 3, 2, 8, 128),
         jacobian.reshape(2, 8, 128),
+        conserved,
+        metric,
         *words,
     )
     return result.reshape(5, 4, 4, 128)

time: 26.8 us -> 27.1 us (1.011)
  Pallas kernels: 26 us -> 26.3 us
where the time goes in v5:
time: 27.1 us; the launch traced here: 26.9 us
  Pallas kernels  26.3 us (97%)
  local copies, waits for them, and re-layouts  0.62 us (2%)
    pallas_call x1, Pallas kernels, local(): pl.pallas_call(functools.partial(kernel, nx, nz), out_shape=pltpu.VMEM((5...  26.3 us
    unnamed x1, local copies, waits for them, and re-layouts  0.62 us

profile of v5, /device:TPU:1, one launch (start us, length us, event | category | flops | bytes accessed | tf_op | source)
XLA Modules:
  0.0 26.9 jit_solution(8742238362300968164)
XLA Ops:
  0.0 26.3 %shard_map.73 = f32[5,2,8,128]{3,2,1,0:T(8,128)S(1)} custom-call(f32[5,2,8,128]{3,2,1,0:T(8,128)} %bitcast.10, f32[3,3,2,8,128]{4,3,2,1,0:T(8,128)} %bitcast.9, f32[2,8,128]{2,1,0:T(8,128)} %bitcast.11, f32[5,4,4,128]{3,2,1,0:T(4,128)} %cons_f.1, f32[3,3,4,4,128]{4,3,2,1,0:T(4,128)} %met_f.1, s32[2,32]{1,0:T(2,128)} %bitcast.12, s32[2,32]{1,0:T(2,128)} %bitcast.13, ...), custom_call_target="tpu_custom_call" | custom-call | tf_op jit(solution)/shard_map/pallas_call | solution.py:500
  26.3 0.6 %copy.9 = f32[5,4,4,128]{3,2,1,0:T(4,128)} copy(f32[5,4,4,128]{3,2,1,0:T(4,128)S(1)} %bitcast.8) | data formatting | bytes 81920

commit v6 on v4

--- a/solution.py
+++ b/solution.py
@@ -108,7 +108,7 @@
     target = lambda way: (x_to[way[0] + 1], z_to[way[1] + 1])
 
     loads = [(ref, codes.at[n]) for n, ref in enumerate((xm, xf, zm, zf))]
-    loads += [(cons_n, nodes), (met_n, metv), (jac_n, jacv)]
+    loads += [(cons_n, nodes), (met_n.at[0:2], metv.at[0:2]), (met_n.at[2], metv.at[2]), (jac_n, jacv)]
     loads = [pltpu.make_async_copy(a, b, csem.at[n]) for n, (a, b) in enumerate(loads)]
     for copy in loads:
         copy.start()
@@ -227,6 +227,8 @@
             parts.append(along(layer, lane_three[axis], 1))
         return jnp.stack(parts)
 
+    cross_row, cross_lane = crossed(row_out[0]), crossed(lane_three[0])
+
     loads[4].wait()
     state = [nodes[k] for k in range(5)]
     velocity, pressure, warm = primitives(state)
@@ -235,14 +237,15 @@
     own_warm = to_faces(warm)
     own_lifted = own_velocity + [own_warm]
     loads[5].wait()
-    metric = [[metv[g, d] for d in range(3)] for g in range(3)]
+    metric = [[metv[g, d] for d in range(3)] for g in range(2)]
     own_row = [
         jnp.stack([to_faces(metric[0][d])[0], to_faces(metric[1][d])[1]]) for d in range(3)
     ]
-    seen = [orient(v, row_out) for v in own_lifted + [lead * own_row[d] for d in range(3)]]
+    shown = own_lifted + [lead * own_row[d] for d in range(3)]
+    shown = [[along(v[axis], lane_one[axis], 1) for axis in range(2)] for v in shown]
     for k in range(7):
-        edge[0, k] = crossed(seen[k][0])
-        edge[1, k] = seen[k][1]
+        edge[0, k] = along(along(shown[k][0], cross_row, 0), cross_lane, 1)
+        edge[1, k] = along(along(shown[k][1], row_out[1], 0), lane_three[1], 1)
 
     corner_sends = []
     for n, way in enumerate(diagonals):
@@ -259,17 +262,23 @@
         )
     corner_sends[0].start()
     corner_sends[2].start()
+    seen = [
+        jnp.stack([along(along(v[0], row_out[0], 0), lane_three[0], 1), edge[1, k]])
+        for k, v in enumerate(shown)
+    ]
 
     def products(g):
         return (lifted[:, None] * jnp.stack(metric[g])[None]).reshape(12, 2, 8, 128)
 
+    loads[6].wait()
+    loads[7].wait()
+    metric.append([metv[2, d] for d in range(3)])
     partial = d_x(products(0)) + d_z(products(1)) + d_y(products(2))
     y_normal = [along(metric[2][d], y_lead, 1) for d in range(3)]
     y_sums = [
         y_side * (lifted[k] + (wall_sign if k < 3 else 1.0) * along(lifted[k], y_other, 1))
         for k in range(4)
     ]
-    loads[6].wait()
     inverse_j = 1.0 / jacv[...]
     scaled = visc_coef * inverse_j
     partial = [
@@ -462,7 +471,7 @@
             pltpu.VMEM((2, 7, 8, 128), jnp.float32),
             pltpu.VMEM((2, 7, 8, 128), jnp.float32),
             pltpu.VMEM((4, 2, 32), jnp.int32),
-            pltpu.SemaphoreType.DMA((7,)),
+            pltpu.SemaphoreType.DMA((8,)),
             pltpu.SemaphoreType.DMA((8,)),
             pltpu.SemaphoreType.DMA((8,)),
             pltpu.SemaphoreType.REGULAR,

time: 26.2 us -> 26.1 us (level)
  no operation moved by 1% of the time
where the time goes in v6:
time: 26.1 us; the launch traced here: 25.9 us
  Pallas kernels  25.3 us (97%)
  local copies, waits for them, and re-layouts  0.62 us (2%)
    pallas_call x1, Pallas kernels, local(): pl.pallas_call(functools.partial(kernel, nx, nz), out_shape=pltpu.VMEM((5...  25.3 us
    unnamed x1, local copies, waits for them, and re-layouts  0.62 us

profile of v6, /device:TPU:1, one launch (start us, length us, event | category | flops | bytes accessed | tf_op | source)
XLA Modules:
  0.0 25.9 jit_solution(2943635952528260819)
XLA Ops:
  0.0 25.3 %shard_map.73 = f32[5,2,8,128]{3,2,1,0:T(8,128)S(1)} custom-call(f32[5,2,8,128]{3,2,1,0:T(8,128)} %bitcast.10, f32[3,3,2,8,128]{4,3,2,1,0:T(8,128)} %bitcast.9, f32[2,8,128]{2,1,0:T(8,128)} %bitcast.11, s32[2,32]{1,0:T(2,128)} %bitcast.12, s32[2,32]{1,0:T(2,128)} %bitcast.13, s32[2,32]{1,0:T(2,128)} %bitcast.14, s32[2,32]{1,0:T(2,128)} %bitcast.15), custom_call_target="tpu_custom_call" | custom-call | tf_op jit(solution)/shard_map/pallas_call | solution.py:460
  25.3 0.6 %copy.9 = f32[5,4,4,128]{3,2,1,0:T(4,128)} copy(f32[5,4,4,128]{3,2,1,0:T(4,128)S(1)} %bitcast.8) | data formatting | bytes 81920
